TPU v7x, 32 devices: a whole 2x2x4 slice. The times are simulated.
32 devices in a mesh: gx: 8 (over z, y), gy: 4 (over x, core).
Axes of the slice: x: 2, y: 2, z: 4, core: 2. Of those that a mesh axis runs over, the one named last changes fastest.
Arguments:
- members_state: float32 [3, 64, 64, 512], P(None, None, 'gx', 'gy'), may hold values from -6 to 6
- depth_level: int32 [64, 512], P('gx', 'gy'), may hold values from 1 to 8
- land_mask: int32 [64, 512], P('gx', 'gy'), may hold values 0 or 1
- obs_cells: int32 [8, 4, 256], P('gx', 'gy'), may hold values from 0 to 1023
- obs_values: float32 [8, 4, 256], P('gx', 'gy'), may hold values from -6 to 6
- obs_error: float32 [8, 4, 256], P('gx', 'gy'), may hold values from 2 to 8
Outputs:
- analysis: float32 [3, 64, 64, 512], P(None, None, 'gx', 'gy')
Inputs may be any that keep to these rules, and one draw needn't show every extreme that they name: Each value of obs_cells is the row-major index of a cell within the 8 x 128 block held by the device at the same position along gx and gy.
All inputs are finite; a program needn't handle non-finite values. No bound on the sum of `land_mask` on one device may be relied on, other than what follows from the above.
Results may differ from a plain program's by a relative error of at most 0.00005.
Values sent between devices are 32-bit elements; how exact they have to be, the bound alone decides.
A program may use at most 64 MiB of HBM per device.

v0:
```python
import jax
import jax.numpy as jnp
from jax import lax
from jax.sharding import PartitionSpec as P


def extended(block, sides, width):
    for axis, dim in sides:
        count = lax.axis_size(axis)
        forward = [(i, i + 1) for i in range(count - 1)]
        backward = [(target, source) for source, target in forward]
        low = lax.ppermute(
            lax.slice_in_dim(block, block.shape[dim] - width, None, axis=dim), axis, forward
        )
        high = lax.ppermute(lax.slice_in_dim(block, 0, width, axis=dim), axis, backward)
        block = jnp.concatenate([low, block, high], axis=dim)
    return block


def height_tendency(padded, geo):
    h = padded[0]
    u = padded[1]
    v = padded[2]
    depth = geo[0]
    mask = geo[1][1:-1, 1:-1]
    east = depth * u
    north = depth * v

    def along_x(a):
        return (a[:, 2:, 1:-1] - a[:, :-2, 1:-1]) * 0.5

    def along_y(a):
        return (a[:, 1:-1, 2:] - a[:, 1:-1, :-2]) * 0.5

    def laplace(a):
        return (
            a[:, 2:, 1:-1]
            + a[:, :-2, 1:-1]
            + a[:, 1:-1, 2:]
            + a[:, 1:-1, :-2]
            - 4.0 * a[:, 1:-1, 1:-1]
        )

    def inner(a):
        return a[:, 1:-1, 1:-1]

    dh = -along_x(east) - along_y(north) + 0.05 * laplace(h)
    du = -along_x(h) + 0.2 * inner(v) + 0.05 * laplace(u)
    dv = -along_y(h) - 0.2 * inner(u) + 0.05 * laplace(v)
    return jnp.stack([dh, du, dv]) * mask


def tri_solve(lower, rhs, flipped):
    return lax.linalg.triangular_solve(lower, rhs, left_side=True, lower=True, transpose_a=flipped)


def padded_section(field):
    return extended(field, (("gx", 2), ("gy", 3)), 1)


def local(members_state, depth_level, land_mask, obs_cells, obs_values, obs_error):
    maskf = land_mask.astype(jnp.float32)
    geo = jnp.stack([0.25 * depth_level.astype(jnp.float32) * maskf, maskf])
    geo_wide = extended(geo, (("gx", 1), ("gy", 2)), 3)
    first_offset = members_state * maskf
    single_geometry = geo_wide[:, 2:-2, 2:-2]
    s1 = first_offset + 0.3 * height_tendency(padded_section(first_offset), single_geometry)
    variance_estimate2 = 0.75 * first_offset + 0.25 * (
        s1 + 0.3 * height_tendency(padded_section(s1), single_geometry)
    )
    prior_model_vector = 1.0 / 3.0 * first_offset + 2.0 / 3.0 * (
        variance_estimate2
        + 0.3 * height_tendency(padded_section(variance_estimate2), single_geometry)
    )
    sample_average = jnp.mean(prior_model_vector, axis=1, keepdims=True)
    sample_deviations = prior_model_vector - sample_average
    sample_number = prior_model_vector.shape[1]
    free_elevation_field = prior_model_vector[0].reshape(sample_number, -1)
    measured_data = jnp.take(free_elevation_field, obs_cells.reshape(-1), axis=1)
    obs_mean = jnp.mean(measured_data, axis=0, keepdims=True)
    error = obs_error.reshape(-1)
    scaled = (measured_data - obs_mean) / (error * jnp.sqrt(jnp.float32(sample_number - 1)))
    innovation = (obs_values.reshape(-1) - obs_mean[0]) / error
    gram_part = jnp.dot(scaled, scaled.T, precision=lax.Precision.HIGHEST)
    proj_part = jnp.dot(scaled, innovation, precision=lax.Precision.HIGHEST)
    eye = jnp.eye(sample_number, dtype=jnp.float32)
    gram, projection = lax.psum((gram_part, proj_part), ("gx", "gy"))
    lower = jnp.linalg.cholesky(eye + gram)
    half = tri_solve(lower, projection[:, None], False)
    weights = tri_solve(lower, half, True)[:, 0]
    inverse = tri_solve(lower, eye, False)
    transform = weights[:, None] / jnp.sqrt(jnp.float32(sample_number - 1)) + inverse.T
    mixed = jnp.einsum(
        "km,fkxy->fmxy", transform, sample_deviations, precision=lax.Precision.HIGHEST
    )
    return sample_average + mixed


def solution(mesh):
    placed = (
        P(None, None, "gx", "gy"),
        P("gx", "gy"),
        P("gx", "gy"),
        P("gx", "gy", None),
        P("gx", "gy", None),
        P("gx", "gy", None),
    )
    return jax.shard_map(
        local, mesh=mesh, in_specs=placed, out_specs=P(None, None, "gx", "gy"), check_vma=False
    )
```

profile of v0, /device:TPU:0, one launch (start us, length us, event | category | flops | bytes accessed | tf_op | source)
XLA Modules:
  0.0 144.8 jit_solution(973424417270132449)
XLA Ops:
  0.0 0.7 convert_bitcast_fusion
  0.7 0.7 multiply_bitcast_fusion
  1.4 1.3 collective-permute-start.1
  2.7 5.5 %collective-permute-start = (f32[2,3,128]{2,1,0:T(4,128)S(1)}, f32[2,3,128]{2,1,0:T(4,128)S(1)}, u32[]{:S(2)}, u32[]{:S(2)}) collective-permute-start(f32[2,3,128]{2,1,0:T(4,128)S(1)} %get-tuple-element.46), channel_id=1, source_target_pairs={{0,4},{4,8},{8,12},{12,16},{16,20},{20,24},{24,28},{1,5},{5,9},{9,... | collective-permute-start | bytes 9224 | tf_op jit(solution)/shard_map/ppermute | solution.py:12
  8.2 1.6 %copy.15 = f32[3,64,8,128]{1,3,2,0:T(8,128)S(1)} copy(f32[3,64,8,128]{3,2,1,0:T(8,128)} %param.6) | data formatting | bytes 1572864 | tf_op args[0]
  9.8 0.2 broadcast_multiply_fusion
  10.2 1.3 collective-permute-start.3
  11.5 3.0 %collective-permute-start.2 = (f32[2,14,3]{2,1,0:T(8,128)S(1)}, f32[2,14,3]{2,1,0:T(8,128)S(1)}, u32[]{:S(2)}, u32[]{:S(2)}) collective-permute-start(f32[2,14,3]{2,1,0:T(8,128)S(1)} %get-tuple-element.44), channel_id=1, source_target_pairs={{0,1},{1,2},{2,3},{4,5},{5,6},{6,7},{8,9},{9,10},{10,11},{12,13},{... | collective-permute-start | bytes 1016 | tf_op jit(solution)/shard_map/ppermute | solution.py:12
  14.5 1.3 collective-permute-start.5
  15.8 5.5 %collective-permute-start.4 = (f32[3,64,1,128]{1,3,2,0:T(8,128)S(1)}, f32[3,64,1,128]{1,3,2,0:T(8,128)S(1)}, u32[]{:S(2)}, u32[]{:S(2)}) collective-permute-start(f32[3,64,1,128]{1,3,2,0:T(8,128)S(1)} %get-tuple-element.40), channel_id=1, source_target_pairs={{0,4},{4,8},{8,12},{12,16},{16,20},{20,24},{24,28},{1,5},{5,9},{9,... | collective-permute-start | bytes 294920 | tf_op jit(solution)/shard_map/ppermute | solution.py:12
  21.3 0.1 pad_maximum_fusion.3
  21.4 3.3 %collective-permute-done.5 = f32[3,64,1,128]{1,3,2,0:T(8,128)S(1)} collective-permute-done((f32[3,64,1,128]{1,3,2,0:T(8,128)S(1)}, f32[3,64,1,128]{1,3,2,0:T(8,128)S(1)}, u32[]{:S(2)}, u32[]{:S(2)}) %collective-permute-start.5) | collective-permute-done | bytes 98336 | tf_op jit(solution)/shard_map/ppermute | solution.py:15
  24.8 5.0 %collective-permute-done.4 = f32[3,64,1,128]{1,3,2,0:T(8,128)S(1)} collective-permute-done((f32[3,64,1,128]{1,3,2,0:T(8,128)S(1)}, f32[3,64,1,128]{1,3,2,0:T(8,128)S(1)}, u32[]{:S(2)}, u32[]{:S(2)}) %collective-permute-start.4) | collective-permute-done | bytes 98336 | tf_op jit(solution)/shard_map/ppermute | solution.py:12
  29.8 1.3 collective-permute-start.7
  31.1 3.0 %collective-permute-start.6 = (f32[3,64,10,1]{1,3,2,0:T(1,128)S(1)}, f32[3,64,10,1]{1,3,2,0:T(1,128)S(1)}, u32[]{:S(2)}, u32[]{:S(2)}) collective-permute-start(f32[3,64,10,1]{1,3,2,0:T(1,128)S(1)} %get-tuple-element.34), channel_id=1, source_target_pairs={{0,1},{1,2},{2,3},{4,5},{5,6},{6,7},{8,9},{9,10},{10,11},{12,13},{... | collective-permute-start | bytes 23048 | tf_op jit(solution)/shard_map/ppermute | solution.py:12
  34.1 0.1 slice_bitcast_fusion.9
  34.3 0.7 collective-permute-done.6
  34.9 0.2 pad_maximum_fusion
  35.2 0.1 slice_bitcast_fusion.6
  35.3 0.2 broadcast_multiply_fusion.6
  35.6 0.6 fusion.60
  36.2 0.4 fusion.64
  36.6 0.4 fusion.1
  37.0 1.3 collective-permute-start.9
  38.3 5.0 %collective-permute-start.8 = (f32[3,64,1,128]{1,3,2,0:T(8,128)S(1)}, f32[3,64,1,128]{1,3,2,0:T(8,128)S(1)}, u32[]{:S(2)}, u32[]{:S(2)}) collective-permute-start(f32[3,64,1,128]{1,3,2,0:T(8,128)S(1)} %get-tuple-element.38), channel_id=1, source_target_pairs={{0,4},{4,8},{8,12},{12,16},{16,20},{20,24},{24,28},{1,5},{5,9},{9,... | collective-permute-start | bytes 294920 | tf_op jit(solution)/shard_map/ppermute | solution.py:12
  43.3 3.2 %collective-permute-done.9 = f32[3,64,1,128]{1,3,2,0:T(8,128)S(1)} collective-permute-done((f32[3,64,1,128]{1,3,2,0:T(8,128)S(1)}, f32[3,64,1,128]{1,3,2,0:T(8,128)S(1)}, u32[]{:S(2)}, u32[]{:S(2)}) %collective-permute-start.9) | collective-permute-done | bytes 98336 | tf_op jit(solution)/shard_map/ppermute | solution.py:15
  46.5 5.2 %collective-permute-done.8 = f32[3,64,1,128]{1,3,2,0:T(8,128)S(1)} collective-permute-done((f32[3,64,1,128]{1,3,2,0:T(8,128)S(1)}, f32[3,64,1,128]{1,3,2,0:T(8,128)S(1)}, u32[]{:S(2)}, u32[]{:S(2)}) %collective-permute-start.8) | collective-permute-done | bytes 98336 | tf_op jit(solution)/shard_map/ppermute | solution.py:12
  51.8 1.3 collective-permute-start.11
  53.1 3.0 %collective-permute-start.10 = (f32[3,64,10,1]{1,3,2,0:T(1,128)S(1)}, f32[3,64,10,1]{1,3,2,0:T(1,128)S(1)}, u32[]{:S(2)}, u32[]{:S(2)}) collective-permute-start(f32[3,64,10,1]{1,3,2,0:T(1,128)S(1)} %get-tuple-element.32), channel_id=1, source_target_pairs={{0,1},{1,2},{2,3},{4,5},{5,6},{6,7},{8,9},{9,10},{10,11},{12,13},{... | collective-permute-start | bytes 23048 | tf_op jit(solution)/shard_map/ppermute | solution.py:12
  56.2 0.8 collective-permute-done.10
  56.9 0.3 pad_maximum_fusion.1
  57.2 0.1 slice_bitcast_fusion.3
  57.4 0.2 broadcast_multiply_fusion.4
  57.6 0.6 fusion.44
  58.2 0.4 fusion.48
  58.6 0.8 fusion.5
  59.4 1.3 collective-permute-start.13
  60.7 5.0 %collective-permute-start.12 = (f32[3,64,1,128]{1,3,2,0:T(8,128)S(1)}, f32[3,64,1,128]{1,3,2,0:T(8,128)S(1)}, u32[]{:S(2)}, u32[]{:S(2)}) collective-permute-start(f32[3,64,1,128]{1,3,2,0:T(8,128)S(1)} %get-tuple-element.36), channel_id=1, source_target_pairs={{0,4},{4,8},{8,12},{12,16},{16,20},{20,24},{24,28},{1,5},{5,9},{9,... | collective-permute-start | bytes 294920 | tf_op jit(solution)/shard_map/ppermute | solution.py:12
  65.8 3.1 %collective-permute-done.13 = f32[3,64,1,128]{1,3,2,0:T(8,128)S(1)} collective-permute-done((f32[3,64,1,128]{1,3,2,0:T(8,128)S(1)}, f32[3,64,1,128]{1,3,2,0:T(8,128)S(1)}, u32[]{:S(2)}, u32[]{:S(2)}) %collective-permute-start.13) | collective-permute-done | bytes 98336 | tf_op jit(solution)/shard_map/ppermute | solution.py:15
  68.9 5.2 %collective-permute-done.12 = f32[3,64,1,128]{1,3,2,0:T(8,128)S(1)} collective-permute-done((f32[3,64,1,128]{1,3,2,0:T(8,128)S(1)}, f32[3,64,1,128]{1,3,2,0:T(8,128)S(1)}, u32[]{:S(2)}, u32[]{:S(2)}) %collective-permute-start.12) | collective-permute-done | bytes 98336 | tf_op jit(solution)/shard_map/ppermute | solution.py:12
  74.2 1.3 collective-permute-start.15
  75.5 3.0 %collective-permute-start.14 = (f32[3,64,10,1]{1,3,2,0:T(1,128)S(1)}, f32[3,64,10,1]{1,3,2,0:T(1,128)S(1)}, u32[]{:S(2)}, u32[]{:S(2)}) collective-permute-start(f32[3,64,10,1]{1,3,2,0:T(1,128)S(1)} %get-tuple-element.30), channel_id=1, source_target_pairs={{0,1},{1,2},{2,3},{4,5},{5,6},{6,7},{8,9},{9,10},{10,11},{12,13},{... | collective-permute-start | bytes 23048 | tf_op jit(solution)/shard_map/ppermute | solution.py:12
  78.6 0.8 collective-permute-done.14
  79.4 0.2 pad_maximum_fusion.2
  79.6 0.1 slice_bitcast_fusion
  79.7 0.2 broadcast_multiply_fusion.2
  80.0 0.6 fusion.28
  80.6 0.4 fusion.32
  81.0 1.7 %fusion.77 = (f32[3,8,128]{2,1,0:T(8,128)S(1)}, f32[3,64,8,128]{1,3,2,0:T(8,128)S(1)}) fusion(f32[8,128]{1,0:T(8,128)S(1)} %slice.421, f32[1,64,8,128]{1,3,2,0:T(8,128)S(1)} %get-tuple-element.16, f32[1,64,8,128]{1,3,2,0:T(8,128)S(1)} %get-tuple-element.15, f32[1,64,8,128]{1,3,2,0:T(8,128)S(1)} %fusion.32, f32[1,64,8,128]{1,3,2,0:T(8,128)S(1)} %get-tuple-element.21, ...), kind=kLoop, calls=%fused_computation.162 | loop fusion | flops 4518912 | bytes 3952640 | tf_op jit(solution)/shard_map/reduce_sum | solution.py:75
  82.8 0.7 gather_fusion
  83.5 0.2 select_reduce_fusion
  83.7 0.2 subtract_divide_fusion
  83.9 0.4 fusion.83
  84.3 0.2 convolution_bitcast_fusion.2
  84.5 44.1 %all-reduce = (f32[64,64]{1,0:T(8,128)S(1)}, f32[64]{0:T(128)S(1)}) all-reduce(f32[64,64]{1,0:T(8,128)S(1)} %fusion.83, f32[64]{0:T(128)S(1)} %convolution_bitcast_fusion.2), channel_id=1, replica_groups=mesh['gx'=8,'gy'=4] {'gx','gy'}, use_global_device_ids=true, to_apply=%region_2.3 | all-reduce | flops 4160 | bytes 33280 | tf_op jit(solution)/shard_map/psum | solution.py:87
  128.6 5.8 %cholesky.18 = f32[64,64]{1,0:T(8,128)S(1)} custom-call(f32[64,64]{1,0:T(8,128)S(1)} %fusion.74), custom_call_target="Cholesky" | custom-call | tf_op jit(solution)/shard_map/jit(cholesky)/cholesky | solution.py:88
  134.5 0.6 compare_reduce_fusion
  135.2 0.7 fusion.70
  135.8 4.9 %custom-call.10 = f32[1,64,64]{1,2,0:T(8,128)S(1)} custom-call(f32[1,64,64]{2,1,0:T(8,128)S(1)} %fusion.70), custom_call_target="InvertDiagBlocksLowerTriangular" | custom-call | tf_op jit(solution)/shard_map/triangular_solve | solution.py:54
  140.7 0.2 convolution_bitcast_fusion.1
  140.9 0.2 fusion.19
  141.0 0.2 fusion.18
  141.3 2.1 %fusion.15 = f32[3,64,8,128]{3,1,2,0:T(8,128)S(1)} fusion(f32[64,64,1,1]{1,0,3,2:T(8,128)S(1)} %fusion.18, f32[3,64,8,128]{1,3,2,0:T(8,128)S(1)} %get-tuple-element.8, f32[3,8,128]{2,1,0:T(8,128)S(1)} %broadcast_multiply_fusion.7), kind=kOutput, calls=%fused_computation.20 | convolution fusion | flops 151388160 | bytes 1601536 | tf_op jit(solution)/shard_map/km,fkxy->fmxy/dot_general | solution.py:93
  143.4 1.3 copy.19
  (33 shorter events, 0.6 us)
Async XLA Ops:
  1.4 8.7 %collective-permute-start.1 = (f32[2,3,128]{2,1,0:T(4,128)S(1)}, f32[2,3,128]{2,1,0:T(4,128)S(1)}, u32[]{:S(2)}, u32[]{:S(2)}) collective-permute-start(f32[2,3,128]{2,1,0:T(4,128)S(1)} %get-tuple-element.47), channel_id=1, source_target_pairs={{4,0},{8,4},{12,8},{16,12},{20,16},{24,20},{28,24},{5,1},{9,5},{13... | collective-permute-start | bytes 9224 | tf_op jit(solution)/shard_map/ppermute | solution.py:15
  2.7 7.4 %collective-permute-start = (f32[2,3,128]{2,1,0:T(4,128)S(1)}, f32[2,3,128]{2,1,0:T(4,128)S(1)}, u32[]{:S(2)}, u32[]{:S(2)}) collective-permute-start(f32[2,3,128]{2,1,0:T(4,128)S(1)} %get-tuple-element.46), channel_id=1, source_target_pairs={{0,4},{4,8},{8,12},{12,16},{16,20},{20,24},{24,28},{1,5},{5,9},{9,... | collective-permute-start | bytes 9224 | tf_op jit(solution)/shard_map/ppermute | solution.py:12
  10.2 11.1 %collective-permute-start.3 = (f32[2,14,3]{2,1,0:T(8,128)S(1)}, f32[2,14,3]{2,1,0:T(8,128)S(1)}, u32[]{:S(2)}, u32[]{:S(2)}) collective-permute-start(f32[2,14,3]{2,1,0:T(8,128)S(1)} %get-tuple-element.45), channel_id=1, source_target_pairs={{1,0},{2,1},{3,2},{5,4},{6,5},{7,6},{9,8},{10,9},{11,10},{13,12},{... | collective-permute-start | bytes 1016 | tf_op jit(solution)/shard_map/ppermute | solution.py:15
  11.5 9.9 %collective-permute-start.2 = (f32[2,14,3]{2,1,0:T(8,128)S(1)}, f32[2,14,3]{2,1,0:T(8,128)S(1)}, u32[]{:S(2)}, u32[]{:S(2)}) collective-permute-start(f32[2,14,3]{2,1,0:T(8,128)S(1)} %get-tuple-element.44), channel_id=1, source_target_pairs={{0,1},{1,2},{2,3},{4,5},{5,6},{6,7},{8,9},{9,10},{10,11},{12,13},{... | collective-permute-start | bytes 1016 | tf_op jit(solution)/shard_map/ppermute | solution.py:12
  14.5 10.2 %collective-permute-start.5 = (f32[3,64,1,128]{1,3,2,0:T(8,128)S(1)}, f32[3,64,1,128]{1,3,2,0:T(8,128)S(1)}, u32[]{:S(2)}, u32[]{:S(2)}) collective-permute-start(f32[3,64,1,128]{1,3,2,0:T(8,128)S(1)} %get-tuple-element.41), channel_id=1, source_target_pairs={{4,0},{8,4},{12,8},{16,12},{20,16},{24,20},{28,24},{5,1},{9,5},{13... | collective-permute-start | bytes 294920 | tf_op jit(solution)/shard_map/ppermute | solution.py:15
  15.8 13.9 %collective-permute-start.4 = (f32[3,64,1,128]{1,3,2,0:T(8,128)S(1)}, f32[3,64,1,128]{1,3,2,0:T(8,128)S(1)}, u32[]{:S(2)}, u32[]{:S(2)}) collective-permute-start(f32[3,64,1,128]{1,3,2,0:T(8,128)S(1)} %get-tuple-element.40), channel_id=1, source_target_pairs={{0,4},{4,8},{8,12},{12,16},{16,20},{20,24},{24,28},{1,5},{5,9},{9,... | collective-permute-start | bytes 294920 | tf_op jit(solution)/shard_map/ppermute | solution.py:12
  29.8 4.5 %collective-permute-start.7 = (f32[3,64,10,1]{1,3,2,0:T(1,128)S(1)}, f32[3,64,10,1]{1,3,2,0:T(1,128)S(1)}, u32[]{:S(2)}, u32[]{:S(2)}) collective-permute-start(f32[3,64,10,1]{1,3,2,0:T(1,128)S(1)} %get-tuple-element.35), channel_id=1, source_target_pairs={{1,0},{2,1},{3,2},{5,4},{6,5},{7,6},{9,8},{10,9},{11,10},{13,12},{... | collective-permute-start | bytes 23048 | tf_op jit(solution)/shard_map/ppermute | solution.py:15
  31.1 3.9 %collective-permute-start.6 = (f32[3,64,10,1]{1,3,2,0:T(1,128)S(1)}, f32[3,64,10,1]{1,3,2,0:T(1,128)S(1)}, u32[]{:S(2)}, u32[]{:S(2)}) collective-permute-start(f32[3,64,10,1]{1,3,2,0:T(1,128)S(1)} %get-tuple-element.34), channel_id=1, source_target_pairs={{0,1},{1,2},{2,3},{4,5},{5,6},{6,7},{8,9},{9,10},{10,11},{12,13},{... | collective-permute-start | bytes 23048 | tf_op jit(solution)/shard_map/ppermute | solution.py:12
  37.0 19.2 %copy-start = (s32[1,1,256]{2,1,0:T(1,128)S(1)}, s32[1,1,256]{2,1,0:T(1,128)}, u32[]{:S(2)}) copy-start(s32[1,1,256]{2,1,0:T(1,128)} %param.9) | copy-start | bytes 3076
  37.0 9.5 %collective-permute-start.9 = (f32[3,64,1,128]{1,3,2,0:T(8,128)S(1)}, f32[3,64,1,128]{1,3,2,0:T(8,128)S(1)}, u32[]{:S(2)}, u32[]{:S(2)}) collective-permute-start(f32[3,64,1,128]{1,3,2,0:T(8,128)S(1)} %get-tuple-element.39), channel_id=1, source_target_pairs={{4,0},{8,4},{12,8},{16,12},{20,16},{24,20},{28,24},{5,1},{9,5},{13... | collective-permute-start | bytes 294920 | tf_op jit(solution)/shard_map/ppermute | solution.py:15
  38.3 13.4 %collective-permute-start.8 = (f32[3,64,1,128]{1,3,2,0:T(8,128)S(1)}, f32[3,64,1,128]{1,3,2,0:T(8,128)S(1)}, u32[]{:S(2)}, u32[]{:S(2)}) collective-permute-start(f32[3,64,1,128]{1,3,2,0:T(8,128)S(1)} %get-tuple-element.38), channel_id=1, source_target_pairs={{0,4},{4,8},{8,12},{12,16},{16,20},{20,24},{24,28},{1,5},{5,9},{9,... | collective-permute-start | bytes 294920 | tf_op jit(solution)/shard_map/ppermute | solution.py:12
  51.8 4.4 %collective-permute-start.11 = (f32[3,64,10,1]{1,3,2,0:T(1,128)S(1)}, f32[3,64,10,1]{1,3,2,0:T(1,128)S(1)}, u32[]{:S(2)}, u32[]{:S(2)}) collective-permute-start(f32[3,64,10,1]{1,3,2,0:T(1,128)S(1)} %get-tuple-element.33), channel_id=1, source_target_pairs={{1,0},{2,1},{3,2},{5,4},{6,5},{7,6},{9,8},{10,9},{11,10},{13,12},{... | collective-permute-start | bytes 23048 | tf_op jit(solution)/shard_map/ppermute | solution.py:15
  53.1 3.9 %collective-permute-start.10 = (f32[3,64,10,1]{1,3,2,0:T(1,128)S(1)}, f32[3,64,10,1]{1,3,2,0:T(1,128)S(1)}, u32[]{:S(2)}, u32[]{:S(2)}) collective-permute-start(f32[3,64,10,1]{1,3,2,0:T(1,128)S(1)} %get-tuple-element.32), channel_id=1, source_target_pairs={{0,1},{1,2},{2,3},{4,5},{5,6},{6,7},{8,9},{9,10},{10,11},{12,13},{... | collective-permute-start | bytes 23048 | tf_op jit(solution)/shard_map/ppermute | solution.py:12
  59.4 9.5 %collective-permute-start.13 = (f32[3,64,1,128]{1,3,2,0:T(8,128)S(1)}, f32[3,64,1,128]{1,3,2,0:T(8,128)S(1)}, u32[]{:S(2)}, u32[]{:S(2)}) collective-permute-start(f32[3,64,1,128]{1,3,2,0:T(8,128)S(1)} %get-tuple-element.37), channel_id=1, source_target_pairs={{4,0},{8,4},{12,8},{16,12},{20,16},{24,20},{28,24},{5,1},{9,5},{13... | collective-permute-start | bytes 294920 | tf_op jit(solution)/shard_map/ppermute | solution.py:15
  60.7 13.4 %collective-permute-start.12 = (f32[3,64,1,128]{1,3,2,0:T(8,128)S(1)}, f32[3,64,1,128]{1,3,2,0:T(8,128)S(1)}, u32[]{:S(2)}, u32[]{:S(2)}) collective-permute-start(f32[3,64,1,128]{1,3,2,0:T(8,128)S(1)} %get-tuple-element.36), channel_id=1, source_target_pairs={{0,4},{4,8},{8,12},{12,16},{16,20},{20,24},{24,28},{1,5},{5,9},{9,... | collective-permute-start | bytes 294920 | tf_op jit(solution)/shard_map/ppermute | solution.py:12
  74.2 4.4 %collective-permute-start.15 = (f32[3,64,10,1]{1,3,2,0:T(1,128)S(1)}, f32[3,64,10,1]{1,3,2,0:T(1,128)S(1)}, u32[]{:S(2)}, u32[]{:S(2)}) collective-permute-start(f32[3,64,10,1]{1,3,2,0:T(1,128)S(1)} %get-tuple-element.31), channel_id=1, source_target_pairs={{1,0},{2,1},{3,2},{5,4},{6,5},{7,6},{9,8},{10,9},{11,10},{13,12},{... | collective-permute-start | bytes 23048 | tf_op jit(solution)/shard_map/ppermute | solution.py:15
  75.5 3.9 %collective-permute-start.14 = (f32[3,64,10,1]{1,3,2,0:T(1,128)S(1)}, f32[3,64,10,1]{1,3,2,0:T(1,128)S(1)}, u32[]{:S(2)}, u32[]{:S(2)}) collective-permute-start(f32[3,64,10,1]{1,3,2,0:T(1,128)S(1)} %get-tuple-element.30), channel_id=1, source_target_pairs={{0,1},{1,2},{2,3},{4,5},{5,6},{6,7},{8,9},{9,10},{10,11},{12,13},{... | collective-permute-start | bytes 23048 | tf_op jit(solution)/shard_map/ppermute | solution.py:12
  82.7 1.0 copy-start.1
  82.7 1.0 copy-start.2
where the time goes:
time: 145 us
  blocking collectives  44.1 us (30%)
  starting transfers between devices  43.5 us (30%)
  waiting for transfers between devices  27.4 us (19%)
  other arithmetic  21.6 us (15%)
  local copies, waits for them, and re-layouts  4.53 us (3%)
  matrix products  3.22 us (2%)
    psum x1, blocking collectives, local(): gram, projection = lax.psum((gram_part, proj_part), ('gx', 'gy'))  44.1 us
    ppermute x8, starting transfers between devices, extended(): lax.ppermute(lax.slice_in_dim(block, block.shape[dim] - width, None, axis...  33.1 us
    ppermute x8, waiting for transfers between devices, extended(): lax.ppermute(lax.slice_in_dim(block, block.shape[dim] - width, None, axis...  17.7 us
    ppermute x8, starting transfers between devices, extended(): lax.ppermute(lax.slice_in_dim(block, 0, width, axis=dim), axis, backward)  10.3 us
    ppermute x8, waiting for transfers between devices, extended(): lax.ppermute(lax.slice_in_dim(block, 0, width, axis=dim), axis, backward)  9.67 us
    another operation x3, other arithmetic, local(): lower = jnp.linalg.cholesky(eye + gram)  6.52 us
    another operation x2, other arithmetic, tri_solve(): lax.linalg.triangular_solve(lower, rhs, left_side=True, lower=True, trans...  5.55 us
    another operation x6, other arithmetic, height_tendency(): return jnp.stack([dh, du, dv]) * mask  2.94 us
  transfers between devices with their start and end apart: 16, of which 9 were waited for; matrix products, arithmetic and copies ran while one was open for 1% of the time, Pallas kernels for 0%

commit v1 on v0

v1 whole, which is shorter than its diff:
```python
import functools
import math

import jax
import jax.numpy as jnp
from jax import lax
from jax.experimental import pallas as pl
from jax.experimental.pallas import tpu as pltpu
from jax.sharding import PartitionSpec as P

W = 3
CHUNK = 16
F32 = jnp.float32
HIGH = lax.Precision.HIGHEST
NT = (((1,), (1,)), ((), ()))


def lanes(shape):
    return lax.broadcasted_iota(jnp.int32, shape, 1)


def roll(a, by):
    by = by % a.shape[-1]
    return a if by == 0 else pltpu.roll(a, by, a.ndim - 1)


def pack(rows):
    out = jnp.zeros_like(rows[0])
    slot = lanes(out.shape) // 8
    for x, row in enumerate(rows):
        out = jnp.where(slot == x, roll(row, 8 * x + 4), out)
    return out


def west(c, strip, x):
    return jnp.where(lanes(c.shape) == 0, roll(strip, -(8 * x + 3)), roll(c, 1))


def east(c, strip, x):
    last = c.shape[1] - 1
    return jnp.where(lanes(c.shape) == last, roll(strip, last - (8 * x + 4)), roll(c, -1))


def tendency(c, up, dn, lf, rt, h_up, h_dn, h_lf, h_rt, mask):
    def lap(f):
        return up[f] + dn[f] + lf[f] + rt[f] - 4.0 * c[f]

    dh = -0.5 * (h_dn * dn[1] - h_up * up[1]) - 0.5 * (h_rt * rt[2] - h_lf * lf[2]) + 0.05 * lap(0)
    du = -0.5 * (dn[0] - up[0]) + 0.2 * c[2] + 0.05 * lap(1)
    dv = -0.5 * (rt[0] - lf[0]) - 0.2 * c[1] + 0.05 * lap(2)
    return dh * mask, du * mask, dv * mask


def forecast_kernel(
    ngx, ngy, state, depth, land, cells, values, error,
    anom_out, mean_out, red_out,
    y, z1, z2, geo, hl, hr, k, lk, rk, gk, glk, grk, sgeo, part, pred, got, gxbuf,
    row_s, row_r, col_s, col_r, grow_s, grow_r, gcol_s, gcol_r, ps, pr, xs, xr,
):
    members = state.shape[1] // depth.shape[0]
    cx = depth.shape[0]
    cy = depth.shape[1]
    ext = cx + 2 * W
    nc = members // CHUNK
    gx = lax.axis_index("gx")
    gy = lax.axis_index("gy")
    steps = ngx.bit_length() - 1

    def dev(a, b):
        return (a, b)

    bar = pltpu.get_barrier_semaphore()
    count = 0
    for target in (
        [dev(lax.rem(gx + 1, ngx), gy), dev(lax.rem(gx + ngx - 1, ngx), gy)]
        + [dev(gx, lax.rem(gy + d, ngy)) for d in range(1, ngy)]
        + [dev(gx + (1 << s) * (1 - 2 * (lax.rem(gx // (1 << s), 2))), gy) for s in range(steps)]
    ):
        pl.semaphore_signal(bar, inc=1, device_id=target, device_id_type=pl.DeviceIdType.MESH)
        count += 1

    maskf = land[...].astype(F32)
    heights = 0.25 * depth[...].astype(F32) * maskf
    for x in range(cx):
        geo[x + W, 0] = jnp.broadcast_to(heights[x : x + 1], (8, cy))
        geo[x + W, 1] = jnp.broadcast_to(maskf[x : x + 1], (8, cy))
    for c in range(nc):
        for f in range(3):
            for x in range(cx):
                y[c, x + W, f] = (
                    state[f, pl.ds(c * CHUNK * cx + x, CHUNK, stride=cx), :] * maskf[x : x + 1]
                )

    @pl.when(gx == 0)
    def _():
        y[:, 0:W] = jnp.zeros((nc, W, 3, CHUNK, cy), F32)
        geo[0:W] = jnp.zeros((W, 2, 8, cy), F32)

    @pl.when(gx == ngx - 1)
    def _():
        y[:, cx + W :] = jnp.zeros((nc, W, 3, CHUNK, cy), F32)
        geo[cx + W :] = jnp.zeros((W, 2, 8, cy), F32)

    @pl.when(gy == 0)
    def _():
        lk[...] = jnp.zeros(lk.shape, F32)
        glk[...] = jnp.zeros(glk.shape, F32)

    @pl.when(gy == ngy - 1)
    def _():
        rk[...] = jnp.zeros(rk.shape, F32)
        grk[...] = jnp.zeros(grk.shape, F32)

    pl.semaphore_wait(bar, count)

    def copy(src, dst, s, r, target):
        return pltpu.make_async_remote_copy(
            src_ref=src, dst_ref=dst, send_sem=s, recv_sem=r,
            device_id=target, device_id_type=pl.DeviceIdType.MESH,
        )

    below = dev(lax.rem(gx + 1, ngx), gy)
    above = dev(lax.rem(gx + ngx - 1, ngx), gy)
    right = dev(gx, lax.rem(gy + 1, ngy))
    left = dev(gx, lax.rem(gy + ngy - 1, ngy))
    has_up, has_dn = gx > 0, gx < ngx - 1
    has_lf, has_rt = gy > 0, gy < ngy - 1

    def rows_of(ref, s, r):
        return (
            copy(ref.at[pl.ds(cx, W)], ref.at[pl.ds(0, W)], s.at[0], r.at[0], below),
            copy(ref.at[pl.ds(W, W)], ref.at[pl.ds(cx + W, W)], s.at[1], r.at[1], above),
        )

    def cols_of(src, to_left, to_right, s, r):
        return (
            copy(src, to_left, s.at[0], r.at[0], right),
            copy(src, to_right, s.at[1], r.at[1], left),
        )

    def start(pair, first, second):
        pl.when(first)(lambda: pair[0].start())
        pl.when(second)(lambda: pair[1].start())

    def sent(pair, first, second):
        pl.when(first)(lambda: pair[0].wait_send())
        pl.when(second)(lambda: pair[1].wait_send())

    def received(pair, first, second):
        pl.when(second)(lambda: pair[0].wait_recv())
        pl.when(first)(lambda: pair[1].wait_recv())

    geo_rows = rows_of(geo, grow_s, grow_r)
    geo_cols = cols_of(gk, glk, grk, gcol_s, gcol_r)
    member_rows = [rows_of(y.at[c], row_s.at[c], row_r.at[c]) for c in range(nc)]
    member_cols = [cols_of(k.at[c], lk.at[c], rk.at[c], col_s.at[c], col_r.at[c]) for c in range(nc)]
    start(geo_rows, has_dn, has_up)
    for c in range(nc):
        start(member_rows[c], has_dn, has_up)

    root = math.sqrt(members - 1)
    err = error[...]
    cell = cells[...]
    obs = cell.shape[1]
    weight = 1.0 / (err * err * root)
    row_at = cell // cy
    col_at = cell - row_at * cy
    sub = lax.broadcasted_iota(jnp.int32, (cx, obs), 0)
    here = sub == row_at
    by_row = jnp.concatenate(
        [jnp.where(here, weight, 0.0), jnp.where(here, weight * values[...], 0.0)], axis=0
    )
    hot = (lax.broadcasted_iota(jnp.int32, (cy, obs), 0) == col_at).astype(F32)
    sums = lax.dot_general(by_row, hot, NT, precision=HIGH, preferred_element_type=F32)
    s_cell, v_cell = sums[:cx], sums[cx:]

    received(geo_rows, has_dn, has_up)
    for f in range(2):
        gk[f] = pack([geo[x, f] for x in range(ext)])
    start(geo_cols, has_rt, has_lf)

    def strips(c):
        received(member_rows[c], has_dn, has_up)
        for f in range(3):
            k[c, f] = pack([y[c, x, f] for x in range(ext)])
        start(member_cols[c], has_rt, has_lf)

    def sections(c):
        received(member_cols[c], has_rt, has_lf)
        first = lanes((CHUNK, cy)) % 8 < 4
        sl0 = [jnp.where(first, lk[c, f], k[c, f]) for f in range(3)]
        sr0 = [jnp.where(first, k[c, f], rk[c, f]) for f in range(3)]

        def strip_section(s, side):
            return tendency(
                s, [roll(a, 8) for a in s], [roll(a, -8) for a in s],
                [roll(a, 1) for a in s], [roll(a, -1) for a in s],
                sgeo[side, 0, 0:1], sgeo[side, 1, 0:1], sgeo[side, 2, 0:1], sgeo[side, 3, 0:1],
                sgeo[side, 4, 0:1],
            )

        def advance(s, side):
            d = strip_section(s, side)
            one = [s[f] + 0.3 * d[f] for f in range(3)]
            d = strip_section(one, side)
            two = [0.75 * s[f] + 0.25 * (one[f] + 0.3 * d[f]) for f in range(3)]
            return one, two

        sl1, sl2 = advance(sl0, 0)
        sr1, sr2 = advance(sr0, 1)

        def row_section(read, sl, sr, x):
            cc, up, dn = read(x), read(x - 1), read(x + 1)
            lf = [west(cc[f], sl[f], x) for f in range(3)]
            rt = [east(cc[f], sr[f], x) for f in range(3)]
            d = tendency(
                cc, up, dn, lf, rt, geo[x - 1, 0, 0:1], geo[x + 1, 0, 0:1],
                hl[x, 0:1], hr[x, 0:1], geo[x, 1, 0:1],
            )
            return cc, d

        for x in range(1, ext - 1):
            cc, d = row_section(lambda i: [y[c, i, f] for f in range(3)], sl0, sr0, x)
            for f in range(3):
                z1[x, f] = cc[f] + 0.3 * d[f]
        for x in range(2, ext - 2):
            cc, d = row_section(lambda i: [z1[i, f] for f in range(3)], sl1, sr1, x)
            for f in range(3):
                z2[x, f] = 0.75 * y[c, x, f] + 0.25 * (cc[f] + 0.3 * d[f])
        for x in range(3, ext - 3):
            cc, d = row_section(lambda i: [z2[i, f] for f in range(3)], sl2, sr2, x)
            for f in range(3):
                anom_out[f, x - W, c * CHUNK : (c + 1) * CHUNK] = (1.0 / 3.0) * y[c, x, f] + (
                    2.0 / 3.0
                ) * (cc[f] + 0.3 * d[f])

    strips(0)
    received(geo_cols, has_rt, has_lf)
    first = lanes((8, cy)) % 8 < 4
    gl = [jnp.where(first, glk[f], gk[f]) for f in range(2)]
    gr = [jnp.where(first, gk[f], grk[f]) for f in range(2)]
    for side, g in ((0, gl), (1, gr)):
        sgeo[side, 0] = roll(g[0], 8)
        sgeo[side, 1] = roll(g[0], -8)
        sgeo[side, 2] = roll(g[0], 1)
        sgeo[side, 3] = roll(g[0], -1)
        sgeo[side, 4] = g[1]
    for x in range(ext):
        hl[x] = west(geo[x, 0], gl[0], x)
        hr[x] = east(geo[x, 0], gr[0], x)
    for c in range(nc):
        if c + 1 < nc:
            strips(c + 1)
        sections(c)

    gram = jnp.zeros((members + 8, members), F32)
    for f in range(3):
        for x in range(cx):
            full = anom_out[f, x]
            mean = jnp.sum(full, axis=0, keepdims=True) * (1.0 / members)
            mean_out[f, x : x + 1] = mean
            full = full - mean
            anom_out[f, x] = full
            if f == 0:
                wide = full * (s_cell[x : x + 1] * (1.0 / root))
                proj = jnp.broadcast_to(v_cell[x : x + 1] - s_cell[x : x + 1] * mean, (8, cy))
                lhs = jnp.concatenate([wide, proj], axis=0)
                gram += lax.dot_general(lhs, full, NT, precision=HIGH, preferred_element_type=F32)
    half = members // 2
    part[0:half] = jnp.concatenate([gram[:half], gram[half:members]], axis=1)
    part[half:] = jnp.concatenate([gram[members:], gram[members:]], axis=1)

    across = [
        copy(part, got.at[ngy - d - 1], ps.at[d - 1], pr.at[ngy - d - 1], dev(gx, lax.rem(gy + d, ngy)))
        for d in range(1, ngy)
    ]
    for d in across:
        d.start()
    for d in across:
        d.wait_recv()
    total = jnp.zeros(part.shape, F32)
    for b in range(ngy):
        term = part[...]
        for e in range(1, ngy):
            term = jnp.where(lax.rem(gy + e, ngy) == b, got[e - 1], term)
        total = total + term
    for d in across:
        d.wait_send()
    for s in range(steps):
        pred[s] = total
        partner = gx + (1 << s) * (1 - 2 * lax.rem(gx // (1 << s), 2))
        swap = copy(pred.at[s], gxbuf.at[s], xs.at[s], xr.at[s], dev(partner, gy))
        swap.start()
        swap.wait()
        total = total + gxbuf[s]
    red_out[...] = total

    sent(geo_rows, has_dn, has_up)
    sent(geo_cols, has_rt, has_lf)
    for c in range(nc):
        sent(member_rows[c], has_dn, has_up)
        sent(member_cols[c], has_rt, has_lf)


PIVOTS = 4


def analysis_kernel(anom, mean, red, out):
    members = anom.shape[2]
    cx = anom.shape[1]
    half = members // 2
    wide = 2 * members
    packed = red[0:half]
    gram = jnp.concatenate([packed, roll(packed, members)], axis=0)
    lane = lanes((members, wide))
    row = lax.broadcasted_iota(jnp.int32, (members, wide), 0)
    aug = jnp.where(lane < members, gram, 0.0)
    aug = jnp.where((lane == row) | (lane == row + members), aug + 1.0, aug)
    tiles = [aug[8 * t : 8 * t + 8] for t in range(members // 8)]
    sub = lax.broadcasted_iota(jnp.int32, (8, wide), 0)
    for k0 in range(0, members, PIVOTS):
        t0, o = k0 // 8, k0 % 8
        cols = {
            t: [jnp.broadcast_to(tiles[t][:, k0 + j : k0 + j + 1], (8, wide)) for j in range(PIVOTS)]
            for t in range(t0, len(tiles))
        }
        rows = [tiles[t0][o + i : o + i + 1] for i in range(PIVOTS)]
        piv = [[cols[t0][j][o + i : o + i + 1] for j in range(PIVOTS)] for i in range(PIVOTS)]
        inv = []
        for j in range(PIVOTS):
            inv.append(1.0 / piv[j][j])
            for i in range(j + 1, PIVOTS):
                m = piv[i][j] * inv[j]
                rows[i] = rows[i] - m * rows[j]
                for q in range(j + 1, PIVOTS):
                    piv[i][q] = piv[i][q] - m * piv[j][q]
        for t in range(t0, len(tiles)):
            cur = cols[t]
            new = tiles[t]
            for j in range(PIVOTS):
                m = cur[j] * inv[j]
                if t == t0:
                    m = jnp.where(sub >= o + PIVOTS, m, 0.0)
                new = new - m * rows[j]
                for q in range(j + 1, PIVOTS):
                    cur[q] = cur[q] - m * piv[j][q]
            if t == t0:
                for i in range(PIVOTS):
                    new = jnp.where(sub == o + i, rows[i] * lax.rsqrt(piv[i][i]), new)
            tiles[t] = new
    linv = roll(jnp.concatenate(tiles, axis=0), members)[:, :members]
    proj = red[half : half + 1, :members]
    first = jnp.sum(linv * proj, axis=1, keepdims=True)
    weights = jnp.sum(linv * first, axis=0, keepdims=True)
    mix = linv + weights * (1.0 / math.sqrt(members - 1))
    for f in range(3):
        for x in range(cx):
            res = jnp.dot(mix, anom[f, x], precision=HIGH, preferred_element_type=F32)
            out[f, pl.ds(x, members, stride=cx), :] = res + mean[f, x : x + 1]


def local(ngx, ngy, members_state, depth_level, land_mask, obs_cells, obs_values, obs_error):
    _, members, cx, cy = members_state.shape
    obs = obs_cells.shape[-1]
    ext = cx + 2 * W
    nc = members // CHUNK
    steps = ngx.bit_length() - 1
    rows = members // 2 + 8
    vmem = pl.BlockSpec(memory_space=pltpu.VMEM)
    dma = pltpu.SemaphoreType.DMA
    anom, mean, red = pl.pallas_call(
        functools.partial(forecast_kernel, ngx, ngy),
        out_shape=(
            jax.ShapeDtypeStruct((3, cx, members, cy), F32),
            jax.ShapeDtypeStruct((3, cx, cy), F32),
            jax.ShapeDtypeStruct((rows, cy), F32),
        ),
        in_specs=[vmem] * 6,
        out_specs=(vmem,) * 3,
        scratch_shapes=[
            pltpu.VMEM((nc, ext, 3, CHUNK, cy), F32),
            pltpu.VMEM((ext, 3, CHUNK, cy), F32),
            pltpu.VMEM((ext, 3, CHUNK, cy), F32),
            pltpu.VMEM((ext, 2, 8, cy), F32),
            pltpu.VMEM((ext, 8, cy), F32),
            pltpu.VMEM((ext, 8, cy), F32),
            pltpu.VMEM((nc, 3, CHUNK, cy), F32),
            pltpu.VMEM((nc, 3, CHUNK, cy), F32),
            pltpu.VMEM((nc, 3, CHUNK, cy), F32),
            pltpu.VMEM((2, 8, cy), F32),
            pltpu.VMEM((2, 8, cy), F32),
            pltpu.VMEM((2, 8, cy), F32),
            pltpu.VMEM((2, 5, 8, cy), F32),
            pltpu.VMEM((rows, cy), F32),
            pltpu.VMEM((steps, rows, cy), F32),
            pltpu.VMEM((ngy - 1, rows, cy), F32),
            pltpu.VMEM((steps, rows, cy), F32),
            dma((nc, 2)), dma((nc, 2)), dma((nc, 2)), dma((nc, 2)),
            dma((2,)), dma((2,)), dma((2,)), dma((2,)),
            dma((ngy - 1,)), dma((ngy - 1,)), dma((steps,)), dma((steps,)),
        ],
        compiler_params=pltpu.CompilerParams(
            collective_id=0, has_side_effects=True, vmem_limit_bytes=40 * 2**20
        ),
    )(
        members_state.reshape(3, members * cx, cy), depth_level, land_mask,
        obs_cells.reshape(1, obs), obs_values.reshape(1, obs), obs_error.reshape(1, obs),
    )
    out = pl.pallas_call(
        analysis_kernel,
        out_shape=jax.ShapeDtypeStruct((3, members * cx, cy), F32),
        in_specs=[vmem] * 3,
        out_specs=vmem,
        compiler_params=pltpu.CompilerParams(vmem_limit_bytes=40 * 2**20),
    )(anom, mean, red)
    return out.reshape(members_state.shape)


def solution(mesh):
    placed = (
        P(None, None, "gx", "gy"),
        P("gx", "gy"),
        P("gx", "gy"),
        P("gx", "gy", None),
        P("gx", "gy", None),
        P("gx", "gy", None),
    )
    return jax.shard_map(
        functools.partial(local, mesh.shape["gx"], mesh.shape["gy"]),
        mesh=mesh, in_specs=placed, out_specs=P(None, None, "gx", "gy"), check_vma=False,
    )
```

time: 145 us -> 42.6 us (0.29)
  blocking collectives: 44.1 us -> 0 us
  starting transfers between devices: 43.5 us -> 0 us
  Pallas kernels: 0 us -> 39.9 us
  waiting for transfers between devices: 27.4 us -> 0 us
  other arithmetic: 21.6 us -> 0 us
  matrix products: 3.22 us -> 0 us
  local copies, waits for them, and re-layouts: 4.53 us -> 2.54 us
    psum x1 -> x0, blocking collectives: 44.1 us -> none  [local(): gram, projection = lax.psum((gram_part, proj_part), ('gx', 'gy'))]
    ppermute x16 -> x0, starting transfers between devices: 43.5 us -> none  [the longest x8 33.1 us: extended(): lax.ppermute(lax.slice_in_dim(block, block.shape[dim] - width, None, axis...]
    pallas_call x0 -> x2, Pallas kernels: none -> 39.9 us  [the longest x1 36 us: local(): pl.pallas_call(functools.partial(forecast_kernel, ngx, ngy), out_shape=(j...]
    ppermute x16 -> x0, waiting for transfers between devices: 27.4 us -> none  [the longest x8 17.7 us: extended(): lax.ppermute(lax.slice_in_dim(block, block.shape[dim] - width, None, axis...]
    another operation x14 -> x0, other arithmetic: 16.4 us -> none  [the longest x3 6.52 us: local(): lower = jnp.linalg.cholesky(eye + gram)]
    dot_general x3 -> x0, matrix products: 2.66 us -> none  [the longest x1 2.11 us: local(): jnp.einsum('km,fkxy->fmxy', transform, sample_deviations, precision=lax.P...]
    reduce_sum x2 -> x0, other arithmetic: 1.89 us -> none  [the longest x1 1.71 us: local(): sample_average = jnp.mean(prior_model_vector, axis=1, keepdims=True)]
  transfers between devices with their start and end apart: 16 -> 0, of which waited for: 9 -> 0; matrix products, arithmetic and copies ran while one was open for 1% -> 0% of each run, Pallas kernels for 0% -> 0%
where the time goes in v1:
time: 42.6 us; the launch traced here: 42.4 us
  Pallas kernels  39.9 us (94%)
  local copies, waits for them, and re-layouts  2.54 us (6%)
    pallas_call x1, Pallas kernels, local(): pl.pallas_call(functools.partial(forecast_kernel, ngx, ngy), out_shape=(j...  36 us
    pallas_call x1, Pallas kernels, local(): pl.pallas_call(analysis_kernel, out_shape=jax.ShapeDtypeStruct((3, member...  3.86 us
    unnamed x12, local copies, waits for them, and re-layouts  2.54 us

profile of v1, /device:TPU:0, one launch (start us, length us, event | category | flops | bytes accessed | tf_op | source)
XLA Modules:
  0.0 42.4 jit_solution(15661588130901947929)
XLA Ops:
  0.0 0.0 copy-start.1
  0.0 0.0 copy-start.4
  0.0 0.0 copy-start.5
  0.0 0.0 copy-start.3
  0.0 0.7 %copy-done.1 = s32[8,128]{1,0:T(8,128)S(1)} copy-done((s32[8,128]{1,0:T(8,128)S(1)}, s32[8,128]{1,0:T(8,128)}, u32[]{:S(2)}) %copy-start.1) | copy-done | bytes 4120
  0.7 0.0 copy-done.4
  0.7 0.0 copy-done.5
  0.7 0.0 copy-done.3
  0.7 0.0 copy-start
  0.7 1.1 %copy-done = f32[3,64,8,128]{3,2,1,0:T(8,128)S(1)} copy-done((f32[3,64,8,128]{3,2,1,0:T(8,128)S(1)}, f32[3,64,8,128]{3,2,1,0:T(8,128)}, u32[]{:S(2)}) %copy-start) | copy-done | bytes 786456
  1.9 0.0 copy-start.2
  1.9 0.7 %copy-done.2 = s32[8,128]{1,0:T(8,128)S(1)} copy-done((s32[8,128]{1,0:T(8,128)S(1)}, s32[8,128]{1,0:T(8,128)}, u32[]{:S(2)}) %copy-start.2) | copy-done | bytes 4120
  2.5 36.0 %shard_map.64 = (f32[3,8,64,128]{3,2,1,0:T(8,128)S(1)}, f32[3,8,128]{2,1,0:T(8,128)S(1)}, f32[40,128]{1,0:T(8,128)S(1)}) custom-call(f32[3,512,128]{2,1,0:T(8,128)S(1)} %bitcast.5, s32[8,128]{1,0:T(8,128)S(1)} %copy-done.1, s32[8,128]{1,0:T(8,128)S(1)} %copy-done.2, s32[1,256]{1,0:T(1,128)S(1)} %bitcast.6, f32[1,256]{1,0:T(1,128)S(1)} %bitcast.7, ...), custom_call_target="tpu_custom_call" | custom-call | tf_op jit(solution)/shard_map/pallas_call | solution.py:371
  38.6 3.9 %shard_map.65 = f32[3,512,128]{2,1,0:T(8,128)} custom-call(f32[3,8,64,128]{3,2,1,0:T(8,128)S(1)} %get-tuple-element.8.anom, f32[3,8,128]{2,1,0:T(8,128)S(1)} %get-tuple-element.9.mean, f32[40,128]{1,0:T(8,128)S(1)} %get-tuple-element.10.red), custom_call_target="tpu_custom_call" | custom-call | tf_op jit(solution)/shard_map/pallas_call | solution.py:409
Async XLA Ops:
  0.0 0.7 %copy-start.1 = (s32[8,128]{1,0:T(8,128)S(1)}, s32[8,128]{1,0:T(8,128)}, u32[]{:S(2)}) copy-start(s32[8,128]{1,0:T(8,128)} %depth.1) | copy-start | bytes 12292
  0.0 0.7 %copy-start.4 = (f32[1,1,256]{2,1,0:T(1,128)S(1)}, f32[1,1,256]{2,1,0:T(1,128)}, u32[]{:S(2)}) copy-start(f32[1,1,256]{2,1,0:T(1,128)} %param.10) | copy-start | bytes 3076
  0.0 0.7 %copy-start.5 = (f32[1,1,256]{2,1,0:T(1,128)S(1)}, f32[1,1,256]{2,1,0:T(1,128)}, u32[]{:S(2)}) copy-start(f32[1,1,256]{2,1,0:T(1,128)} %param.11) | copy-start | bytes 3076
  0.0 0.7 %copy-start.3 = (s32[1,1,256]{2,1,0:T(1,128)S(1)}, s32[1,1,256]{2,1,0:T(1,128)}, u32[]{:S(2)}) copy-start(s32[1,1,256]{2,1,0:T(1,128)} %param.9) | copy-start | bytes 3076
  0.7 1.1 %copy-start = (f32[3,64,8,128]{3,2,1,0:T(8,128)S(1)}, f32[3,64,8,128]{3,2,1,0:T(8,128)}, u32[]{:S(2)}) copy-start(f32[3,64,8,128]{3,2,1,0:T(8,128)} %param.6) | copy-start | bytes 2359300
  1.9 0.7 %copy-start.2 = (s32[8,128]{1,0:T(8,128)S(1)}, s32[8,128]{1,0:T(8,128)}, u32[]{:S(2)}) copy-start(s32[8,128]{1,0:T(8,128)} %land.1) | copy-start | bytes 12292

commit v2 on v1

--- a/solution.py
+++ b/solution.py
@@ -84,12 +84,13 @@
     for x in range(cx):
         geo[x + W, 0] = jnp.broadcast_to(heights[x : x + 1], (8, cy))
         geo[x + W, 1] = jnp.broadcast_to(maskf[x : x + 1], (8, cy))
-    for c in range(nc):
+
+    @pl.loop(0, nc)
+    def _(c):
         for f in range(3):
             for x in range(cx):
-                y[c, x + W, f] = (
-                    state[f, pl.ds(c * CHUNK * cx + x, CHUNK, stride=cx), :] * maskf[x : x + 1]
-                )
+                at = pl.ds(c * CHUNK * cx + x, CHUNK, stride=cx)
+                y[c, x + W, f] = state[f, at, :] * maskf[x : x + 1]
 
     @pl.when(gx == 0)
     def _():
@@ -152,11 +153,18 @@
 
     geo_rows = rows_of(geo, grow_s, grow_r)
     geo_cols = cols_of(gk, glk, grk, gcol_s, gcol_r)
-    member_rows = [rows_of(y.at[c], row_s.at[c], row_r.at[c]) for c in range(nc)]
-    member_cols = [cols_of(k.at[c], lk.at[c], rk.at[c], col_s.at[c], col_r.at[c]) for c in range(nc)]
+
+    def member_rows(c):
+        return rows_of(y.at[c], row_s.at[c], row_r.at[c])
+
+    def member_cols(c):
+        return cols_of(k.at[c], lk.at[c], rk.at[c], col_s.at[c], col_r.at[c])
+
     start(geo_rows, has_dn, has_up)
-    for c in range(nc):
-        start(member_rows[c], has_dn, has_up)
+
+    @pl.loop(0, nc)
+    def _(c):
+        start(member_rows(c), has_dn, has_up)
 
     root = math.sqrt(members - 1)
     err = error[...]
@@ -180,13 +188,13 @@
     start(geo_cols, has_rt, has_lf)
 
     def strips(c):
-        received(member_rows[c], has_dn, has_up)
+        received(member_rows(c), has_dn, has_up)
         for f in range(3):
             k[c, f] = pack([y[c, x, f] for x in range(ext)])
-        start(member_cols[c], has_rt, has_lf)
+        start(member_cols(c), has_rt, has_lf)
 
     def sections(c):
-        received(member_cols[c], has_rt, has_lf)
+        received(member_cols(c), has_rt, has_lf)
         first = lanes((CHUNK, cy)) % 8 < 4
         sl0 = [jnp.where(first, lk[c, f], k[c, f]) for f in range(3)]
         sr0 = [jnp.where(first, k[c, f], rk[c, f]) for f in range(3)]
@@ -230,7 +238,7 @@
         for x in range(3, ext - 3):
             cc, d = row_section(lambda i: [z2[i, f] for f in range(3)], sl2, sr2, x)
             for f in range(3):
-                anom_out[f, x - W, c * CHUNK : (c + 1) * CHUNK] = (1.0 / 3.0) * y[c, x, f] + (
+                anom_out[f, x - W, pl.ds(pl.multiple_of(c * CHUNK, CHUNK), CHUNK)] = (1.0 / 3.0) * y[c, x, f] + (
                     2.0 / 3.0
                 ) * (cc[f] + 0.3 * d[f])
 
@@ -248,9 +256,10 @@
     for x in range(ext):
         hl[x] = west(geo[x, 0], gl[0], x)
         hr[x] = east(geo[x, 0], gr[0], x)
-    for c in range(nc):
-        if c + 1 < nc:
-            strips(c + 1)
+
+    @pl.loop(0, nc)
+    def _(c):
+        pl.when(c + 1 < nc)(lambda: strips(c + 1))
         sections(c)
 
     gram = jnp.zeros((members + 8, members), F32)
@@ -297,9 +306,11 @@
 
     sent(geo_rows, has_dn, has_up)
     sent(geo_cols, has_rt, has_lf)
-    for c in range(nc):
-        sent(member_rows[c], has_dn, has_up)
-        sent(member_cols[c], has_rt, has_lf)
+
+    @pl.loop(0, nc)
+    def _(c):
+        sent(member_rows(c), has_dn, has_up)
+        sent(member_cols(c), has_rt, has_lf)
 
 
 PIVOTS = 4

time: 42.6 us -> 43.2 us (1.014)
  Pallas kernels: 39.9 us -> 40.4 us
    pallas_call x1, Pallas kernels: 36 us -> 36.6 us  [local(): pl.pallas_call(functools.partial(forecast_kernel, ngx, ngy), out_shape=(j...]
where the time goes in v2:
time: 43.2 us; the launch traced here: 43 us
  Pallas kernels  40.4 us (94%)
  local copies, waits for them, and re-layouts  2.54 us (6%)
    pallas_call x1, Pallas kernels, local(): pl.pallas_call(functools.partial(forecast_kernel, ngx, ngy), out_shape=(j...  36.6 us
    pallas_call x1, Pallas kernels, local(): pl.pallas_call(analysis_kernel, out_shape=jax.ShapeDtypeStruct((3, member...  3.86 us
    unnamed x12, local copies, waits for them, and re-layouts  2.54 us

profile of v2, /device:TPU:0, one launch (start us, length us, event | category | flops | bytes accessed | tf_op | source)
XLA Modules:
  0.0 43.0 jit_solution(12331784115770079267)
XLA Ops:
  0.0 0.0 copy-start.1
  0.0 0.0 copy-start.4
  0.0 0.0 copy-start.5
  0.0 0.0 copy-start.3
  0.0 0.7 %copy-done.1 = s32[8,128]{1,0:T(8,128)S(1)} copy-done((s32[8,128]{1,0:T(8,128)S(1)}, s32[8,128]{1,0:T(8,128)}, u32[]{:S(2)}) %copy-start.1) | copy-done | bytes 4120
  0.7 0.0 copy-done.4
  0.7 0.0 copy-done.5
  0.7 0.0 copy-done.3
  0.7 0.0 copy-start
  0.7 1.1 %copy-done = f32[3,64,8,128]{3,2,1,0:T(8,128)S(1)} copy-done((f32[3,64,8,128]{3,2,1,0:T(8,128)S(1)}, f32[3,64,8,128]{3,2,1,0:T(8,128)}, u32[]{:S(2)}) %copy-start) | copy-done | bytes 786456
  1.9 0.0 copy-start.2
  1.9 0.7 %copy-done.2 = s32[8,128]{1,0:T(8,128)S(1)} copy-done((s32[8,128]{1,0:T(8,128)S(1)}, s32[8,128]{1,0:T(8,128)}, u32[]{:S(2)}) %copy-start.2) | copy-done | bytes 4120
  2.5 36.6 %shard_map.64 = (f32[3,8,64,128]{3,2,1,0:T(8,128)S(1)}, f32[3,8,128]{2,1,0:T(8,128)S(1)}, f32[40,128]{1,0:T(8,128)S(1)}) custom-call(f32[3,512,128]{2,1,0:T(8,128)S(1)} %bitcast.5, s32[8,128]{1,0:T(8,128)S(1)} %copy-done.1, s32[8,128]{1,0:T(8,128)S(1)} %copy-done.2, s32[1,256]{1,0:T(1,128)S(1)} %bitcast.6, f32[1,256]{1,0:T(1,128)S(1)} %bitcast.7, ...), custom_call_target="tpu_custom_call" | custom-call | tf_op jit(solution)/shard_map/pallas_call | solution.py:382
  39.1 3.9 %shard_map.65 = f32[3,512,128]{2,1,0:T(8,128)} custom-call(f32[3,8,64,128]{3,2,1,0:T(8,128)S(1)} %get-tuple-element.8.anom, f32[3,8,128]{2,1,0:T(8,128)S(1)} %get-tuple-element.9.mean, f32[40,128]{1,0:T(8,128)S(1)} %get-tuple-element.10.red), custom_call_target="tpu_custom_call" | custom-call | tf_op jit(solution)/shard_map/pallas_call | solution.py:420
Async XLA Ops:
  0.0 0.7 %copy-start.1 = (s32[8,128]{1,0:T(8,128)S(1)}, s32[8,128]{1,0:T(8,128)}, u32[]{:S(2)}) copy-start(s32[8,128]{1,0:T(8,128)} %depth.1) | copy-start | bytes 12292
  0.0 0.7 %copy-start.4 = (f32[1,1,256]{2,1,0:T(1,128)S(1)}, f32[1,1,256]{2,1,0:T(1,128)}, u32[]{:S(2)}) copy-start(f32[1,1,256]{2,1,0:T(1,128)} %param.10) | copy-start | bytes 3076
  0.0 0.7 %copy-start.5 = (f32[1,1,256]{2,1,0:T(1,128)S(1)}, f32[1,1,256]{2,1,0:T(1,128)}, u32[]{:S(2)}) copy-start(f32[1,1,256]{2,1,0:T(1,128)} %param.11) | copy-start | bytes 3076
  0.0 0.7 %copy-start.3 = (s32[1,1,256]{2,1,0:T(1,128)S(1)}, s32[1,1,256]{2,1,0:T(1,128)}, u32[]{:S(2)}) copy-start(s32[1,1,256]{2,1,0:T(1,128)} %param.9) | copy-start | bytes 3076
  0.7 1.1 %copy-start = (f32[3,64,8,128]{3,2,1,0:T(8,128)S(1)}, f32[3,64,8,128]{3,2,1,0:T(8,128)}, u32[]{:S(2)}) copy-start(f32[3,64,8,128]{3,2,1,0:T(8,128)} %param.6) | copy-start | bytes 2359300
  1.9 0.7 %copy-start.2 = (s32[8,128]{1,0:T(8,128)S(1)}, s32[8,128]{1,0:T(8,128)}, u32[]{:S(2)}) copy-start(s32[8,128]{1,0:T(8,128)} %land.1) | copy-start | bytes 12292

commit v3 on v1

--- a/solution.py
+++ b/solution.py
@@ -9,7 +9,7 @@
 from jax.sharding import PartitionSpec as P
 
 W = 3
-CHUNK = 16
+CHUNK = 32
 F32 = jnp.float32
 HIGH = lax.Precision.HIGHEST
 NT = (((1,), (1,)), ((), ()))

time: 42.6 us -> 43 us (level)
  no operation moved by 1% of the time
where the time goes in v3:
time: 43 us; the launch traced here: 42.7 us
  Pallas kernels  40.2 us (93%)
  local copies, waits for them, and re-layouts  2.54 us (6%)
    pallas_call x1, Pallas kernels, local(): pl.pallas_call(functools.partial(forecast_kernel, ngx, ngy), out_shape=(j...  36.3 us
    pallas_call x1, Pallas kernels, local(): pl.pallas_call(analysis_kernel, out_shape=jax.ShapeDtypeStruct((3, member...  3.86 us
    unnamed x12, local copies, waits for them, and re-layouts  2.54 us

profile of v3, /device:TPU:0, one launch (start us, length us, event | category | flops | bytes accessed | tf_op | source)
XLA Modules:
  0.0 42.7 jit_solution(8636280899039021097)
XLA Ops:
  0.0 0.0 copy-start.1
  0.0 0.0 copy-start.4
  0.0 0.0 copy-start.5
  0.0 0.0 copy-start.3
  0.0 0.7 %copy-done.1 = s32[8,128]{1,0:T(8,128)S(1)} copy-done((s32[8,128]{1,0:T(8,128)S(1)}, s32[8,128]{1,0:T(8,128)}, u32[]{:S(2)}) %copy-start.1) | copy-done | bytes 4120
  0.7 0.0 copy-done.4
  0.7 0.0 copy-done.5
  0.7 0.0 copy-done.3
  0.7 0.0 copy-start
  0.7 1.1 %copy-done = f32[3,64,8,128]{3,2,1,0:T(8,128)S(1)} copy-done((f32[3,64,8,128]{3,2,1,0:T(8,128)S(1)}, f32[3,64,8,128]{3,2,1,0:T(8,128)}, u32[]{:S(2)}) %copy-start) | copy-done | bytes 786456
  1.9 0.0 copy-start.2
  1.9 0.7 %copy-done.2 = s32[8,128]{1,0:T(8,128)S(1)} copy-done((s32[8,128]{1,0:T(8,128)S(1)}, s32[8,128]{1,0:T(8,128)}, u32[]{:S(2)}) %copy-start.2) | copy-done | bytes 4120
  2.5 36.3 %shard_map.64 = (f32[3,8,64,128]{3,2,1,0:T(8,128)S(1)}, f32[3,8,128]{2,1,0:T(8,128)S(1)}, f32[40,128]{1,0:T(8,128)S(1)}) custom-call(f32[3,512,128]{2,1,0:T(8,128)S(1)} %bitcast.5, s32[8,128]{1,0:T(8,128)S(1)} %copy-done.1, s32[8,128]{1,0:T(8,128)S(1)} %copy-done.2, s32[1,256]{1,0:T(1,128)S(1)} %bitcast.6, f32[1,256]{1,0:T(1,128)S(1)} %bitcast.7, ...), custom_call_target="tpu_custom_call" | custom-call | tf_op jit(solution)/shard_map/pallas_call | solution.py:371
  38.9 3.9 %shard_map.65 = f32[3,512,128]{2,1,0:T(8,128)} custom-call(f32[3,8,64,128]{3,2,1,0:T(8,128)S(1)} %get-tuple-element.8.anom, f32[3,8,128]{2,1,0:T(8,128)S(1)} %get-tuple-element.9.mean, f32[40,128]{1,0:T(8,128)S(1)} %get-tuple-element.10.red), custom_call_target="tpu_custom_call" | custom-call | tf_op jit(solution)/shard_map/pallas_call | solution.py:409
Async XLA Ops:
  0.0 0.7 %copy-start.1 = (s32[8,128]{1,0:T(8,128)S(1)}, s32[8,128]{1,0:T(8,128)}, u32[]{:S(2)}) copy-start(s32[8,128]{1,0:T(8,128)} %depth.1) | copy-start | bytes 12292
  0.0 0.7 %copy-start.4 = (f32[1,1,256]{2,1,0:T(1,128)S(1)}, f32[1,1,256]{2,1,0:T(1,128)}, u32[]{:S(2)}) copy-start(f32[1,1,256]{2,1,0:T(1,128)} %param.10) | copy-start | bytes 3076
  0.0 0.7 %copy-start.5 = (f32[1,1,256]{2,1,0:T(1,128)S(1)}, f32[1,1,256]{2,1,0:T(1,128)}, u32[]{:S(2)}) copy-start(f32[1,1,256]{2,1,0:T(1,128)} %param.11) | copy-start | bytes 3076
  0.0 0.7 %copy-start.3 = (s32[1,1,256]{2,1,0:T(1,128)S(1)}, s32[1,1,256]{2,1,0:T(1,128)}, u32[]{:S(2)}) copy-start(s32[1,1,256]{2,1,0:T(1,128)} %param.9) | copy-start | bytes 3076
  0.7 1.1 %copy-start = (f32[3,64,8,128]{3,2,1,0:T(8,128)S(1)}, f32[3,64,8,128]{3,2,1,0:T(8,128)}, u32[]{:S(2)}) copy-start(f32[3,64,8,128]{3,2,1,0:T(8,128)} %param.6) | copy-start | bytes 2359300
  1.9 0.7 %copy-start.2 = (s32[8,128]{1,0:T(8,128)S(1)}, s32[8,128]{1,0:T(8,128)}, u32[]{:S(2)}) copy-start(s32[8,128]{1,0:T(8,128)} %land.1) | copy-start | bytes 12292
